TPU v7x, 512 devices: a whole 4x8x8 slice. The times are simulated.
512 devices in a mesh: grp: 32 (over x, z), vocab: 16 (over y, core).
Axes of the slice: x: 4, y: 8, z: 8, core: 2. Of those that a mesh axis runs over, the one named last changes fastest.
Arguments:
- teacher_rows: bfloat16 [64, 8, 4096], P('grp', None, 'vocab'), may hold values from -160 to 160
- student_rows: bfloat16 [32, 8, 5120], P('grp', None, 'vocab'), may hold values from -160 to 160
- teacher_head: bfloat16 [4096, 131072], P(None, ('grp', 'vocab')), may hold values from -0.25 to 0.25
- student_head: bfloat16 [5120, 131072], P(None, ('grp', 'vocab')), may hold values from -0.25 to 0.25
- lengths: int32 [64], replicated, may hold values from 1 to 7, as said below
- owner: int32 [64], replicated, may hold values from 0 to 31, as said below
Outputs:
- divergence: float32 [32, 8], P('grp')
- grad_student: bfloat16 [32, 8, 5120], P('grp', None, 'vocab')
Inputs may be any that keep to these rules, and one draw needn't show every extreme that they name: All 2 sequences of one teacher group share one owner, and each student group owns the sequences of exactly one teacher group. The lengths of the 2 sequences of one teacher group sum to at most 8, and to exactly 8 for some group.
All inputs are finite; a program needn't handle non-finite values.
Results may differ from a plain program's by a relative error of at most 0.018.
Values may be sent and summed in bfloat16 or wider, within the bound.
No kernel may reach another device: no remote copies, remote signals or barrier semaphores. Data moves between devices by JAX's collectives and lax.ppermute only.
A program may use at most 64 MiB of HBM per device.

v0:
```python
import jax
import jax.numpy as jnp
from jax import lax
from jax.sharding import Mesh
from jax.sharding import PartitionSpec as P

GRP = ("grp_0", "grp_1")
VOCAB = ("vocab_0", "vocab_1")
GRP_VOCAB = ("grp_0", "grp_1", "vocab_0", "vocab_1")


def in_order(pieces, dim):
    pieces = jnp.moveaxis(pieces, 0, dim)
    shape = pieces.shape
    return pieces.reshape(*shape[:dim], shape[dim] * shape[dim + 1], *shape[dim + 2 :])


def one_gather(arrays, axis, dims):
    flat = jnp.concatenate([a.reshape(-1) for a in arrays])
    lines, at, outs = (lax.all_gather(flat, axis), 0, [])
    for a, dim in zip(arrays, dims):
        pieces = lines[:, at : at + a.size].reshape(-1, *a.shape)
        outs.append(in_order(pieces, dim))
        at += a.size
    return tuple(outs)


def stacked_from(shard, axes, sequence):
    pieces = shard
    for k in sequence:
        pieces = lax.all_gather(pieces, axes[k])
    done = sequence[::-1]
    back = [done.index(k) for k in range(len(axes))]
    pieces = pieces.transpose(*back, *range(len(axes), pieces.ndim))
    return pieces.reshape(-1, *shard.shape)


def gathered_by_axis(shard, axes, sequence, dim):
    return in_order(stacked_from(shard, axes, sequence), dim)


def collected_together(shard, axis):
    leaves = jax.tree.leaves(shard)
    sequence = sorted(range(len(leaves)), key=lambda k: -leaves[k].size)
    width = (1, *leaves[sequence[0]].shape)[-1]
    lines = [
        jnp.pad(leaves[k].reshape(-1), (0, -leaves[k].size % width)).reshape(-1, width)
        for k in sequence
    ]
    both, at, found = (lax.all_gather(jnp.concatenate(lines), axis), 0, {})
    for k, line in zip(sequence, lines):
        section = both[:, at : at + len(line)].reshape(len(both), -1)
        found[k] = section[:, : leaves[k].size].reshape(-1, *leaves[k].shape)
        at += len(line)
    numbers = iter(range(len(leaves)))
    return jax.tree.map(lambda _: found[next(numbers)], shard)


def combined_by_axis(shard, axes, combine):
    for axis in axes:
        pieces = collected_together(shard, axis)
        shard = jax.tree.map(lambda part: part[0], pieces)
        for k in range(1, lax.axis_size(axis)):
            shard = combine(shard, jax.tree.map(lambda part: part[k], pieces))
    return shard


def in_blocks(shard, dim, count):
    shape = shard.shape
    pieces = shard.reshape(*shape[:dim], count, shape[dim] // count, *shape[dim + 1 :])
    return jnp.moveaxis(pieces, dim, 0)


def sum_at_owner(shard, axis, dim):
    count = lax.axis_size(axis)
    pieces = lax.all_to_all(in_blocks(shard, dim, count), axis, 0, 0, tiled=True)
    return jnp.sum(pieces.astype(jnp.float32), axis=0)


def routing_tables(lengths, owner, groups, seq_count, positions, pad_rows):
    slot_count = seq_count * positions
    group_ids = jnp.arange(groups, dtype=jnp.int32)
    length_table = lengths.reshape(groups, seq_count)
    owner_table = owner.reshape(groups, seq_count)[:, 0]
    teacher_of = jnp.sum(
        (owner_table[None, :] == group_ids[:, None]).astype(jnp.int32) * group_ids[None, :], axis=1
    )
    position_ids = jnp.arange(positions, dtype=jnp.int32)
    live_slots = (position_ids[None, None, :] < length_table[:, :, None]).reshape(
        groups, slot_count
    )
    ranked = jnp.cumsum(live_slots.astype(jnp.int32), axis=1) - 1
    target = jnp.where(live_slots, ranked, pad_rows)
    matches = target[:, None, :] == jnp.arange(pad_rows, dtype=jnp.int32)[None, :, None]
    source = jnp.sum(
        matches.astype(jnp.int32) * jnp.arange(slot_count, dtype=jnp.int32)[None, None, :], axis=2
    )
    totals = jnp.sum(length_table, axis=1)
    owned_total = jnp.take(totals, teacher_of, axis=0)
    student_live = jnp.arange(pad_rows, dtype=jnp.int32)[None, :] < owned_total[:, None]
    return (teacher_of, source, student_live)


def combine(left_part, right_part):
    teacher_top = jnp.maximum(left_part[0], right_part[0])
    teacher_total = left_part[1] * jnp.exp(left_part[0] - teacher_top) + right_part[1] * jnp.exp(
        right_part[0] - teacher_top
    )
    student_top = jnp.maximum(left_part[2], right_part[2])
    left_scale = jnp.exp(left_part[2] - student_top)
    right_factor = jnp.exp(right_part[2] - student_top)
    student_total = left_part[3] * left_scale + right_part[3] * right_factor
    weighted = left_part[4] * left_scale + right_part[4] * right_factor
    return (teacher_top, teacher_total, student_top, student_total, weighted)


def per_device(teacher_rows, student_rows, teacher_head, student_head, lengths, owner):
    groups = lax.axis_size(GRP)
    seq_count = teacher_rows.shape[0]
    positions = teacher_rows.shape[1]
    slot_count = seq_count * positions
    pad_rows = student_rows.shape[1]
    own_group = lax.axis_index(GRP)
    teacher_of, source, student_live = routing_tables(
        lengths, owner, groups, seq_count, positions, pad_rows
    )
    local_teacher = teacher_rows.reshape(slot_count, teacher_rows.shape[2])
    local_student = student_rows.reshape(pad_rows, student_rows.shape[2])
    own_source = lax.dynamic_index_in_dim(source, own_group, 0, keepdims=False)
    sent_teacher = jnp.take(local_teacher, own_source, axis=0)
    row_position = teacher_of[:, None] * pad_rows + jnp.arange(pad_rows, dtype=jnp.int32)[None, :]
    teacher_full, student_full = one_gather((sent_teacher, local_student), VOCAB, (1, 1))
    raw_teacher = jnp.dot(
        lax.all_gather(teacher_full, GRP, axis=0, tiled=True),
        teacher_head,
        preferred_element_type=jnp.float32,
    )
    student_logits = jnp.dot(
        gathered_by_axis(student_full, GRP, (0, 1), 0),
        student_head,
        preferred_element_type=jnp.float32,
    )
    teacher_logits = jnp.take(raw_teacher, row_position.reshape(-1), axis=0)
    weight = student_live.reshape(-1).astype(jnp.float32)
    local_teacher_top = jnp.max(teacher_logits, axis=1)
    local_student_top = jnp.max(student_logits, axis=1)
    student_exp = jnp.exp(student_logits - local_student_top[:, None])
    merged = combined_by_axis(
        (
            local_teacher_top,
            jnp.sum(jnp.exp(teacher_logits - local_teacher_top[:, None]), axis=1),
            local_student_top,
            jnp.sum(student_exp, axis=1),
            jnp.sum(student_exp * (student_logits - teacher_logits), axis=1),
        ),
        GRP_VOCAB,
        combine,
    )
    teacher_lse = merged[0] + jnp.log(merged[1])
    student_lse = merged[2] + jnp.log(merged[3])
    log_q = student_logits - student_lse[:, None]
    log_p = teacher_logits - teacher_lse[:, None]
    student_prob = jnp.exp(log_q)
    log_ratio = log_q - log_p
    kl_rows = merged[4] / merged[3] - student_lse + teacher_lse
    kl_rows = kl_rows * weight
    grad_logits = (weight[:, None] * student_prob * (log_ratio - kl_rows[:, None])).astype(
        jnp.bfloat16
    )
    partial_value = jnp.einsum(
        "rv,dv->rd", grad_logits, student_head, preferred_element_type=jnp.float32
    )
    feature_totals_acc = sum_at_owner(partial_value.astype(jnp.bfloat16), VOCAB, 1)
    grad_rows = sum_at_owner(feature_totals_acc.astype(jnp.bfloat16), GRP, 0).astype(jnp.bfloat16)
    divergence = lax.dynamic_slice_in_dim(kl_rows, own_group * pad_rows, pad_rows, 0)
    return (divergence.reshape(1, pad_rows), grad_rows.reshape(1, pad_rows, grad_rows.shape[1]))


def solution(mesh):
    torus = Mesh(mesh.devices.reshape(4, 8, 8, 2), ("grp_0", "grp_1", "vocab_0", "vocab_1"))
    return jax.shard_map(
        per_device,
        mesh=torus,
        in_specs=(
            P(GRP, None, VOCAB),
            P(GRP, None, VOCAB),
            P(None, GRP_VOCAB),
            P(None, GRP_VOCAB),
            P(),
            P(),
        ),
        out_specs=(P(GRP, None), P(GRP, None, VOCAB)),
        check_vma=False,
    )
```

profile of v0, /device:TPU:1, one launch (start us, length us, event | category | flops | bytes accessed | tf_op | source)
XLA Modules:
  0.0 332.1 jit_solution(13637512223904512838)
XLA Ops:
  7.2 0.9 reshape.2804
  8.4 0.2 reduce_window_sum.11
  8.7 0.2 dynamic-slice_reduce_fusion
  8.9 0.8 reshape_reshape.6
  9.7 1.3 gather_fusion.1
  11.1 21.7 %all-gather.6 = bf16[16,1,4608]{2,1,0:T(2,128)(2,1)S(1)} all-gather(bf16[1,1,4608]{2,1,0:T(2,128)(2,1)S(1)} %reshape.2848), channel_id=2, replica_groups=mesh['grp_0'=4,'grp_1'=8,'vocab_0'=8,'vocab_1'=2] {'vocab_0','vocab_1'}, dimensions={0}, use_global_device_ids=true | all-gather | bytes 156672 | tf_op jit(solution)/shard_map/all_gather | solution.py:20
  32.8 0.6 copy.45
  33.5 0.1 reshape.2810
  33.7 0.1 all_gather_reshape.3
  33.8 10.2 %all_gather.45 = bf16[4,8,5120]{2,1,0:T(8,128)(2,1)} all-gather(bf16[1,8,5120]{2,1,0:T(8,128)(2,1)S(1)} %all_gather_reshape.3), channel_id=1, replica_groups=mesh['grp_0'=4,'grp_1'=8,'vocab_0'=8,'vocab_1'=2] {'grp_0'}, dimensions={0}, use_global_device_ids=true | all-gather | bytes 409600 | tf_op jit(solution)/shard_map/all_gather | solution.py:31
  44.5 0.7 gather_fusion
  45.7 67.2 %all-gather.14.cloned.1.call-done = bf16[256,4096]{1,0:T(8,128)(2,1)} async-done(((bf16[8,4096]{1,0:T(8,128)(2,1)}), bf16[256,4096]{1,0:T(8,128)(2,1)}) %all-gather.14.cloned.1.call-update) | async-done | bytes 2097168 | tf_op jit(solution)/shard_map/all_gather | solution.py:134
  113.0 2.9 fusion.212
  115.9 1.0 gather_fusion.2
  116.9 0.1 copy.38
  117.1 41.4 %all-gather.16.cloned.1.call-done = bf16[32,8,5120]{2,1,0:T(8,128)(2,1)} async-done(((bf16[4,8,5120]{2,1,0:T(8,128)(2,1)}), bf16[32,8,5120]{2,1,0:T(8,128)(2,1)}) %all-gather.16.cloned.1.call-update) | async-done | bytes 2621456 | tf_op jit(solution)/shard_map/all_gather | solution.py:31
  158.4 1.9 copy.40
  160.4 1.1 fusion.211
  161.5 0.1 multiply_reduce_fusion
  161.7 9.3 %all-gather.7 = f32[4,5,256]{2,1,0:T(8,128)S(1)} all-gather(f32[1,5,256]{2,1,0:T(8,128)S(1)} %bitcast.1105), channel_id=4, replica_groups=mesh['grp_0'=4,'grp_1'=8,'vocab_0'=8,'vocab_1'=2] {'grp_0'}, dimensions={0}, use_global_device_ids=true | all-gather | bytes 25600 | tf_op jit(solution)/shard_map/all_gather | solution.py:50
  171.1 18.3 %all-gather.8 = f32[8,5,256]{2,1,0:T(8,128)S(1)} all-gather(f32[1,5,256]{2,1,0:T(8,128)S(1)} %bitcast.1106), channel_id=5, replica_groups=mesh['grp_0'=4,'grp_1'=8,'vocab_0'=8,'vocab_1'=2] {'grp_1'}, dimensions={0}, use_global_device_ids=true | all-gather | bytes 46080 | tf_op jit(solution)/shard_map/all_gather | solution.py:50
  189.6 19.3 %all-gather.9 = f32[8,5,256]{2,1,0:T(8,128)S(1)} all-gather(f32[1,5,256]{2,1,0:T(8,128)S(1)} %bitcast.1107), channel_id=6, replica_groups=mesh['grp_0'=4,'grp_1'=8,'vocab_0'=8,'vocab_1'=2] {'vocab_0'}, dimensions={0}, use_global_device_ids=true | all-gather | bytes 46080 | tf_op jit(solution)/shard_map/all_gather | solution.py:50
  209.0 20.9 %all-gather.10 = f32[2,5,256]{2,1,0:T(8,128)S(1)} all-gather(f32[1,5,256]{2,1,0:T(8,128)S(1)} %bitcast.1108), channel_id=7, replica_groups=mesh['grp_0'=4,'grp_1'=8,'vocab_0'=8,'vocab_1'=2] {'vocab_1'}, dimensions={0}, use_global_device_ids=true | all-gather | bytes 15360 | tf_op jit(solution)/shard_map/all_gather | solution.py:50
  229.9 2.5 convolution_convert_fusion
  232.4 4.4 %copy.41 = bf16[256,5120]{0,1:T(8,128)(2,1)} copy(bf16[256,5120]{1,0:T(8,128)(2,1)} %convolution_convert_fusion) | data formatting | bytes 5242880 | tf_op jit(solution)/shard_map/convert_element_type | solution.py:173
  236.8 68.4 %all_to_all.10 = bf16[16,256,320]{1,2,0:T(8,128)(2,1)} all-to-all(bf16[16,256,320]{1,2,0:T(8,128)(2,1)} %bitcast.1097), channel_id=1, replica_groups=mesh['grp_0'=4,'grp_1'=8,'vocab_0'=8,'vocab_1'=2] {'vocab_0','vocab_1'}, dimensions={0} | all-to-all | bytes 5242880 | tf_op jit(solution)/shard_map/all_to_all | solution.py:76
  305.1 2.1 reduce_sum.87
  307.3 0.8 copy.42
  308.1 6.0 %all-to-all-start.1 = ((bf16[32,8,320]{2,1,0:T(8,128)(2,1)}), bf16[32,8,320]{2,1,0:T(8,128)(2,1)S(1)}, u32[]{:S(2)}, u32[]{:S(2)}) async-start(bf16[32,8,320]{2,1,0:T(8,128)(2,1)} %bitcast.134), calls=%async_computation.1 | async-start | bytes 393216 | tf_op jit(solution)/shard_map/all_to_all | solution.py:76
  314.1 0.6 dynamic-slice_bitcast_fusion
  314.7 10.0 %all-to-all-done.1 = bf16[32,8,320]{2,1,0:T(8,128)(2,1)S(1)} async-done(((bf16[32,8,320]{2,1,0:T(8,128)(2,1)}), bf16[32,8,320]{2,1,0:T(8,128)(2,1)S(1)}, u32[]{:S(2)}, u32[]{:S(2)}) %all-to-all-start.1) | async-done | bytes 163872 | tf_op jit(solution)/shard_map/all_to_all | solution.py:76
  324.6 0.6 reduce_sum.88
  (59 shorter events, 2.1 us)
Async XLA Ops:
  7.2 153.2 %copy-start = (bf16[5120,256]{1,0:T(8,128)(2,1)S(1)}, bf16[5120,256]{1,0:T(8,128)(2,1)}, u32[]{:S(2)}) copy-start(bf16[5120,256]{1,0:T(8,128)(2,1)} %param.9) | copy-start | bytes 7864324
  7.2 37.0 %copy-start.1 = (s32[64]{0:T(128)S(1)}, s32[64]{0:T(128)}, u32[]{:S(2)}) copy-start(s32[64]{0:T(128)} %param.11) | copy-start | bytes 772
  7.2 105.8 %all-gather.14.cloned.1.call-start = ((), (), s32[]{:S(2)}) async-start(), calls=%async_computation.2 | async-start | bytes 2162688 | tf_op jit(solution)/shard_map/all_gather | solution.py:134
  33.4 125.0 %all-gather.16.cloned.1.call-start = ((), (), s32[]{:S(2)}) async-start(), calls=%async_computation.3 | async-start | bytes 2949120 | tf_op jit(solution)/shard_map/all_gather | solution.py:31
  308.1 16.6 %all-to-all-start.1 = ((bf16[32,8,320]{2,1,0:T(8,128)(2,1)}), bf16[32,8,320]{2,1,0:T(8,128)(2,1)S(1)}, u32[]{:S(2)}, u32[]{:S(2)}) async-start(bf16[32,8,320]{2,1,0:T(8,128)(2,1)} %bitcast.134), calls=%async_computation.1 | async-start | bytes 393216 | tf_op jit(solution)/shard_map/all_to_all | solution.py:76
Sparse Core Ops, SparseCore 0:
  33.6 79.3 all-gather.13
  115.1 43.3 all-gather.15
where the time goes:
time: 333 us; the launch traced here: 332 us
  blocking collectives  168 us (50%)
  waiting for transfers between devices  119 us (36%)
  local copies, waits for them, and re-layouts  14.5 us (4%)
  between operations  14.3 us (4%)
  matrix products  6.54 us (2%)
  starting transfers between devices  6.08 us (2%)
  other arithmetic  3.99 us (1%)
    all_to_all x1, blocking collectives, sum_at_owner(): lax.all_to_all(in_blocks(shard, dim, count), axis, 0, 0, tiled=True)  68.4 us
    all_gather x4, blocking collectives, collected_together(): both, at, found = (lax.all_gather(jnp.concatenate(lines), axis), 0, {})  67.8 us
    all_gather x1, waiting for transfers between devices, per_device(): lax.all_gather(teacher_full, GRP, axis=0, tiled=True)  67.2 us
    all_gather x1, waiting for transfers between devices, stacked_from(): pieces = lax.all_gather(pieces, axes[k])  41.4 us
    all_gather x1, blocking collectives, one_gather(): lines, at, outs = (lax.all_gather(flat, axis), 0, [])  21.7 us
    all_gather x1, blocking collectives, stacked_from(): pieces = lax.all_gather(pieces, axes[k])  10.2 us
    all_to_all x1, waiting for transfers between devices, sum_at_owner(): lax.all_to_all(in_blocks(shard, dim, count), axis, 0, 0, tiled=True)  9.96 us
  transfers between devices with their start and end apart: 3, of which 3 were waited for; matrix products, arithmetic and copies ran while one was open for 2% of the time, Pallas kernels for 0%

commit v1 on v0

--- a/solution.py
+++ b/solution.py
@@ -131,7 +131,9 @@
     row_position = teacher_of[:, None] * pad_rows + jnp.arange(pad_rows, dtype=jnp.int32)[None, :]
     teacher_full, student_full = one_gather((sent_teacher, local_student), VOCAB, (1, 1))
     raw_teacher = jnp.dot(
-        lax.all_gather(teacher_full, GRP, axis=0, tiled=True),
+        jnp.concatenate(
+            lax.all_to_all(jnp.stack([teacher_full] * lax.axis_size(GRP)), GRP, 0, 0), axis=0
+        ),
         teacher_head,
         preferred_element_type=jnp.float32,
     )

time: 333 us -> 300 us (0.901)
  waiting for transfers between devices: 119 us -> 78 us
  starting transfers between devices: 6.08 us -> 16.9 us
  blocking collectives: 168 us -> 164 us
    all_gather x1 -> x0, waiting for transfers between devices: 67.2 us -> none  [per_device(): lax.all_gather(teacher_full, GRP, axis=0, tiled=True)]
    all_to_all x0 -> x1, waiting for transfers between devices: none -> 59.1 us  [per_device(): lax.all_to_all(jnp.stack([teacher_full] * lax.axis_size(GRP)), GRP, 0, 0)]
    all_gather x1, waiting for transfers between devices: 41.4 us -> 8.83 us  [stacked_from(): pieces = lax.all_gather(pieces, axes[k])]
    all_to_all x0 -> x1, starting transfers between devices: none -> 10.9 us  [per_device(): lax.all_to_all(jnp.stack([teacher_full] * lax.axis_size(GRP)), GRP, 0, 0)]
  transfers between devices with their start and end apart: 3 -> 3, of which waited for: 3 -> 3; matrix products, arithmetic and copies ran while one was open for 2% -> 3% of each run, Pallas kernels for 0% -> 0%
where the time goes in v1:
time: 300 us; the launch traced here: 299 us
  blocking collectives  164 us (55%)
  waiting for transfers between devices  78 us (26%)
  starting transfers between devices  16.9 us (6%)
  local copies, waits for them, and re-layouts  15.5 us (5%)
  between operations  14.3 us (5%)
  matrix products  6.54 us (2%)
  other arithmetic  3.98 us (1%)
    all_to_all x1, blocking collectives, sum_at_owner(): lax.all_to_all(in_blocks(shard, dim, count), axis, 0, 0, tiled=True)  66.9 us
    all_gather x4, blocking collectives, collected_together(): both, at, found = (lax.all_gather(jnp.concatenate(lines), axis), 0, {})  65.3 us
    all_to_all x1, waiting for transfers between devices, per_device(): lax.all_to_all(jnp.stack([teacher_full] * lax.axis_size(GRP)), GRP, 0, 0)  59.1 us
    all_gather x1, blocking collectives, one_gather(): lines, at, outs = (lax.all_gather(flat, axis), 0, [])  21.7 us
    all_to_all x1, starting transfers between devices, per_device(): lax.all_to_all(jnp.stack([teacher_full] * lax.axis_size(GRP)), GRP, 0, 0)  10.9 us
    all_gather x1, blocking collectives, stacked_from(): pieces = lax.all_gather(pieces, axes[k])  10.2 us
    all_to_all x1, waiting for transfers between devices, sum_at_owner(): lax.all_to_all(in_blocks(shard, dim, count), axis, 0, 0, tiled=True)  9.97 us
    all_gather x1, waiting for transfers between devices, stacked_from(): pieces = lax.all_gather(pieces, axes[k])  8.83 us
  transfers between devices with their start and end apart: 3, of which 3 were waited for; matrix products, arithmetic and copies ran while one was open for 3% of the time, Pallas kernels for 0%

profile of v1, /device:TPU:1, one launch (start us, length us, event | category | flops | bytes accessed | tf_op | source)
XLA Modules:
  0.0 299.3 jit_solution(10105985711036775779)
XLA Ops:
  7.3 0.9 reshape.2806
  8.4 0.2 reduce_window_sum.11
  8.7 0.2 dynamic-slice_reduce_fusion
  8.9 0.8 reshape_reshape.6
  9.7 1.3 gather_fusion.1
  11.1 21.7 %all-gather.6 = bf16[16,1,4608]{2,1,0:T(2,128)(2,1)S(1)} all-gather(bf16[1,1,4608]{2,1,0:T(2,128)(2,1)S(1)} %reshape.2850), channel_id=2, replica_groups=mesh['grp_0'=4,'grp_1'=8,'vocab_0'=8,'vocab_1'=2] {'vocab_0','vocab_1'}, dimensions={0}, use_global_device_ids=true | all-gather | bytes 156672 | tf_op jit(solution)/shard_map/all_gather | solution.py:20
  32.8 0.1 reshape.2812
  32.9 0.1 all_gather_reshape.3
  33.1 10.2 %all_gather.41 = bf16[4,8,5120]{2,1,0:T(8,128)(2,1)} all-gather(bf16[1,8,5120]{2,1,0:T(8,128)(2,1)S(1)} %all_gather_reshape.3), channel_id=1, replica_groups=mesh['grp_0'=4,'grp_1'=8,'vocab_0'=8,'vocab_1'=2] {'grp_0'}, dimensions={0}, use_global_device_ids=true | all-gather | bytes 409600 | tf_op jit(solution)/shard_map/all_gather | solution.py:31
  43.4 1.6 stack.3
  45.0 10.9 %all-to-all-start = ((bf16[32,8,4096]{2,1,0:T(8,128)(2,1)}), bf16[32,8,4096]{2,1,0:T(8,128)(2,1)}, u32[]{:S(2)}, u32[]{:S(2)}) async-start(bf16[32,8,4096]{2,1,0:T(8,128)(2,1)} %stack.3), calls=%async_computation | async-start | bytes 4194304 | tf_op jit(solution)/shard_map/all_to_all | solution.py:135
  56.4 0.7 gather_fusion
  57.6 59.1 %all-to-all-done = bf16[32,8,4096]{2,1,0:T(8,128)(2,1)} async-done(((bf16[32,8,4096]{2,1,0:T(8,128)(2,1)}), bf16[32,8,4096]{2,1,0:T(8,128)(2,1)}, u32[]{:S(2)}, u32[]{:S(2)}) %all-to-all-start) | async-done | bytes 2097184 | tf_op jit(solution)/shard_map/all_to_all | solution.py:135
  116.7 2.9 fusion
  119.7 1.0 gather_fusion.2
  120.6 0.1 copy.38
  120.8 8.8 %all-gather.13.cloned.1.call-done = bf16[32,8,5120]{2,1,0:T(8,128)(2,1)} async-done(((bf16[4,8,5120]{2,1,0:T(8,128)(2,1)}), bf16[32,8,5120]{2,1,0:T(8,128)(2,1)}) %all-gather.13.cloned.1.call-update) | async-done | bytes 2621456 | tf_op jit(solution)/shard_map/all_gather | solution.py:31
  129.7 1.9 copy.40
  131.6 1.1 fusion.213
  132.9 9.3 %all-gather.7 = f32[4,5,256]{2,1,0:T(8,128)S(1)} all-gather(f32[1,5,256]{2,1,0:T(8,128)S(1)} %bitcast.1107), channel_id=4, replica_groups=mesh['grp_0'=4,'grp_1'=8,'vocab_0'=8,'vocab_1'=2] {'grp_0'}, dimensions={0}, use_global_device_ids=true | all-gather | bytes 25600 | tf_op jit(solution)/shard_map/all_gather | solution.py:50
  142.3 18.2 %all-gather.8 = f32[8,5,256]{2,1,0:T(8,128)S(1)} all-gather(f32[1,5,256]{2,1,0:T(8,128)S(1)} %bitcast.1108), channel_id=5, replica_groups=mesh['grp_0'=4,'grp_1'=8,'vocab_0'=8,'vocab_1'=2] {'grp_1'}, dimensions={0}, use_global_device_ids=true | all-gather | bytes 46080 | tf_op jit(solution)/shard_map/all_gather | solution.py:50
  160.7 18.3 %all-gather.9 = f32[8,5,256]{2,1,0:T(8,128)S(1)} all-gather(f32[1,5,256]{2,1,0:T(8,128)S(1)} %bitcast.1109), channel_id=6, replica_groups=mesh['grp_0'=4,'grp_1'=8,'vocab_0'=8,'vocab_1'=2] {'vocab_0'}, dimensions={0}, use_global_device_ids=true | all-gather | bytes 46080 | tf_op jit(solution)/shard_map/all_gather | solution.py:50
  179.1 19.5 %all-gather.10 = f32[2,5,256]{2,1,0:T(8,128)S(1)} all-gather(f32[1,5,256]{2,1,0:T(8,128)S(1)} %bitcast.1110), channel_id=7, replica_groups=mesh['grp_0'=4,'grp_1'=8,'vocab_0'=8,'vocab_1'=2] {'vocab_1'}, dimensions={0}, use_global_device_ids=true | all-gather | bytes 15360 | tf_op jit(solution)/shard_map/all_gather | solution.py:50
  198.7 2.5 convolution_convert_fusion
  201.1 4.4 %copy.41 = bf16[256,5120]{0,1:T(8,128)(2,1)} copy(bf16[256,5120]{1,0:T(8,128)(2,1)} %convolution_convert_fusion) | data formatting | bytes 5242880 | tf_op jit(solution)/shard_map/convert_element_type | solution.py:175
  205.5 66.9 %all_to_all.15 = bf16[16,256,320]{1,2,0:T(8,128)(2,1)} all-to-all(bf16[16,256,320]{1,2,0:T(8,128)(2,1)} %bitcast.1099), channel_id=1, replica_groups=mesh['grp_0'=4,'grp_1'=8,'vocab_0'=8,'vocab_1'=2] {'vocab_0','vocab_1'}, dimensions={0} | all-to-all | bytes 5242880 | tf_op jit(solution)/shard_map/all_to_all | solution.py:76
  272.4 2.1 reduce_sum.87
  274.5 0.8 copy.42
  275.3 5.9 %all-to-all-start.2 = ((bf16[32,8,320]{2,1,0:T(8,128)(2,1)}), bf16[32,8,320]{2,1,0:T(8,128)(2,1)S(1)}, u32[]{:S(2)}, u32[]{:S(2)}) async-start(bf16[32,8,320]{2,1,0:T(8,128)(2,1)} %bitcast.135), calls=%async_computation.2 | async-start | bytes 393216 | tf_op jit(solution)/shard_map/all_to_all | solution.py:76
  281.2 0.6 dynamic-slice_bitcast_fusion
  281.8 10.0 %all-to-all-done.2 = bf16[32,8,320]{2,1,0:T(8,128)(2,1)S(1)} async-done(((bf16[32,8,320]{2,1,0:T(8,128)(2,1)}), bf16[32,8,320]{2,1,0:T(8,128)(2,1)S(1)}, u32[]{:S(2)}, u32[]{:S(2)}) %all-to-all-start.2) | async-done | bytes 163872 | tf_op jit(solution)/shard_map/all_to_all | solution.py:76
  291.8 0.6 reduce_sum.88
  (59 shorter events, 2.1 us)
Async XLA Ops:
  7.2 124.4 %copy-start = (bf16[5120,256]{1,0:T(8,128)(2,1)S(1)}, bf16[5120,256]{1,0:T(8,128)(2,1)}, u32[]{:S(2)}) copy-start(bf16[5120,256]{1,0:T(8,128)(2,1)} %param.9) | copy-start | bytes 7864324
  7.2 122.5 %all-gather.13.cloned.1.call-start = ((), (), s32[]{:S(2)}) async-start(), calls=%async_computation.3 | async-start | bytes 2949120 | tf_op jit(solution)/shard_map/all_gather | solution.py:31
  45.0 11.1 %copy-start.1 = (s32[64]{0:T(128)S(1)}, s32[64]{0:T(128)}, u32[]{:S(2)}) copy-start(s32[64]{0:T(128)} %param.11) | copy-start | bytes 772
  45.0 71.7 %all-to-all-start = ((bf16[32,8,4096]{2,1,0:T(8,128)(2,1)}), bf16[32,8,4096]{2,1,0:T(8,128)(2,1)}, u32[]{:S(2)}, u32[]{:S(2)}) async-start(bf16[32,8,4096]{2,1,0:T(8,128)(2,1)} %stack.3), calls=%async_computation | async-start | bytes 4194304 | tf_op jit(solution)/shard_map/all_to_all | solution.py:135
  275.3 16.5 %all-to-all-start.2 = ((bf16[32,8,320]{2,1,0:T(8,128)(2,1)}), bf16[32,8,320]{2,1,0:T(8,128)(2,1)S(1)}, u32[]{:S(2)}, u32[]{:S(2)}) async-start(bf16[32,8,320]{2,1,0:T(8,128)(2,1)} %bitcast.135), calls=%async_computation.2 | async-start | bytes 393216 | tf_op jit(solution)/shard_map/all_to_all | solution.py:76
Sparse Core Ops, SparseCore 0:
  43.5 86.1 all-gather.12
